TPU v7x, 32 devices: a whole 2x2x4 slice. The times are simulated.
32 devices in a mesh: dp: 8 (over z, core), mp: 4 (over y, x).
Axes of the slice: x: 2, y: 2, z: 4, core: 2. Of those that a mesh axis runs over, the one named last changes fastest.
Arguments:
- inputs: bfloat16 [2, 8, 2308, 1024], P(None, 'dp', 'mp'), may hold values from -6 to 6
- cotangent: bfloat16 [2, 8, 2308, 1024], P(None, 'dp', 'mp'), may hold values from -6 to 6
- counts: int32 [2, 8], P(None, 'dp'), may hold values from 1 to 4, as said below
- qkv_weight: bfloat16 [1024, 3, 1024], P('dp', None, 'mp'), may hold values from -0.1875 to 0.1875
- qv_bias: bfloat16 [2, 1024], P(None, 'mp'), may hold values from -0.75 to 0.75
- out_weight: bfloat16 [1024, 1024], P('mp', 'dp'), may hold values from -1.5 to 1.5
- up_weight: bfloat16 [1024, 4096], P('dp', 'mp'), may hold values from -0.1875 to 0.1875
- up_bias: bfloat16 [4096], P('mp'), may hold values from -4 to 4
- down_weight: bfloat16 [4096, 1024], P('mp', 'dp'), may hold values from -0.09375 to 0.09375
- norm_gain: bfloat16 [2, 1024], P(None, 'dp'), may hold values from 0.099609375 to 1.8984375
- norm_shift: bfloat16 [2, 1024], P(None, 'dp'), may hold values from -4 to 4
- out_bias: bfloat16 [2, 1024], P(None, 'dp'), may hold values from -4 to 4
Outputs:
- outputs: bfloat16 [2, 8, 2308, 1024], P(None, 'dp', 'mp')
- input_grad: float32 [2, 8, 2308, 1024], P(None, 'dp', 'mp')
- qkv_grad: float32 [1024, 3, 1024], P('dp', None, 'mp')
- qv_bias_grad: float32 [2, 1024], P(None, 'mp')
- out_weight_grad: float32 [1024, 1024], P('mp', 'dp')
- up_weight_grad: float32 [1024, 4096], P('dp', 'mp')
- up_bias_grad: float32 [4096], P('mp')
- down_weight_grad: float32 [4096, 1024], P('mp', 'dp')
- norm_gain_grad: float32 [2, 1024], P(None, 'dp')
- norm_shift_grad: float32 [2, 1024], P(None, 'dp')
- out_bias_grad: float32 [2, 1024], P(None, 'dp')
Inputs may be any that keep to these rules, and one draw needn't show every extreme that they name: Slots 0 to counts - 1 of a group hold its images; in each micro-batch some data group holds all 4.
All inputs are finite; a program needn't handle non-finite values.
Results may differ from a plain program's by a relative error of at most 0.02.
Values may be sent and summed in bfloat16 or wider, within the bound.
A program may use at most 448 MiB of HBM per device.

v0:
```python
import jax
import jax.numpy as jnp
from jax import lax
from jax.sharding import PartitionSpec as P

HEAD_DIM = 64
SEQ = 577


norm_eps = 1e-06
half_root = 0.7071067811865476
density_scale = 0.3989422804014327


def transposed_product(left, right):
    return lax.dot_general(
        left, right, (((0,), (0,)), ((), ())), preferred_element_type=jnp.float32
    )


def product_by_transpose(left, right):
    return lax.dot_general(
        left, right, (((1,), (1,)), ((), ())), preferred_element_type=jnp.float32
    )


def normalize(values, gain, shift):
    center = jnp.mean(values, axis=-1, keepdims=True)
    centered = values - center
    spread = jnp.mean(centered * centered, axis=-1, keepdims=True)
    inverse = lax.rsqrt(spread + norm_eps)
    normed = centered * inverse
    return (normed * gain + shift, normed, inverse)


def normalize_back(grad_result, normed, inverse, gain):
    scaled = grad_result * gain
    first_mean = jnp.mean(scaled, axis=-1, keepdims=True)
    second_mean = jnp.mean(scaled * normed, axis=-1, keepdims=True)
    return inverse * (scaled - first_mean - normed * second_mean)


def gelu_slope(values):
    return 0.5 * (1.0 + lax.erf(values * half_root)) + values * density_scale * jnp.exp(
        -0.5 * values * values
    )


def attend(block):
    query = block[:, 0]
    key_block = block[:, 1]
    value = block[:, 2]
    scale = query.shape[-1] ** (-0.5)
    scores = (
        jnp.einsum("qhd,khd->hqk", query, key_block, preferred_element_type=jnp.float32) * scale
    )
    top_score = jnp.max(scores, axis=-1, keepdims=True)
    weights = jnp.exp(scores - top_score)
    totals = jnp.sum(weights, axis=-1, keepdims=True)
    weights_low = (weights / totals).astype(jnp.bfloat16)
    mixed = jnp.einsum(
        "hqk,khd->qhd", weights_low, value, preferred_element_type=jnp.float32
    ).astype(jnp.bfloat16)
    return (mixed, (top_score + jnp.log(totals))[..., 0])


def attend_back(operands):
    block, mixed_grad, log_total = operands
    query = block[:, 0]
    key_block = block[:, 1]
    value = block[:, 2]
    scale = query.shape[-1] ** (-0.5)
    scores = (
        jnp.einsum("qhd,khd->hqk", query, key_block, preferred_element_type=jnp.float32) * scale
    )
    weights = jnp.exp(scores - log_total[..., None])
    weights_low = weights.astype(jnp.bfloat16)
    value_grad = jnp.einsum(
        "hqk,qhd->khd", weights_low, mixed_grad, preferred_element_type=jnp.float32
    ).astype(jnp.bfloat16)
    weight_grad = jnp.einsum("qhd,khd->hqk", mixed_grad, value, preferred_element_type=jnp.float32)
    centre = jnp.sum(weights * weight_grad, axis=-1, keepdims=True)
    score_grad = (weights * (weight_grad - centre)).astype(jnp.bfloat16)
    query_grad = (
        jnp.einsum("hqk,khd->qhd", score_grad, key_block, preferred_element_type=jnp.float32)
        * scale
    ).astype(jnp.bfloat16)
    key_grad = (
        jnp.einsum("hqk,qhd->khd", score_grad, query, preferred_element_type=jnp.float32) * scale
    ).astype(jnp.bfloat16)
    return jnp.stack([query_grad, key_grad, value_grad], axis=1)


def shards(
    inputs,
    cotangent,
    counts,
    qkv_weight,
    qv_bias,
    out_weight,
    up_weight,
    up_bias,
    down_weight,
    norm_gain,
    norm_shift,
    out_bias,
):
    qkv_full, out_full, up_full, down_full, gain_full, shift_full, bias_full = (
        lax.all_gather(qkv_weight, "dp", axis=0, tiled=True),
        lax.all_gather(out_weight, "dp", axis=1, tiled=True),
        lax.all_gather(up_weight, "dp", axis=0, tiled=True),
        lax.all_gather(down_weight, "dp", axis=1, tiled=True),
        lax.all_gather(norm_gain, "dp", axis=1, tiled=True),
        lax.all_gather(norm_shift, "dp", axis=1, tiled=True),
        lax.all_gather(out_bias, "dp", axis=1, tiled=True),
    )
    groups = lax.axis_size("mp")
    width = qkv_full.shape[0]
    local_width = qkv_full.shape[2]
    unit_width = up_full.shape[1]
    qkv_matrix = qkv_full.reshape(width, 3 * local_width)
    gain_wide = gain_full.astype(jnp.float32)
    shift_wide = shift_full.astype(jnp.float32)
    bias_wide = bias_full.astype(jnp.float32)
    head_bias = qv_bias.astype(jnp.float32)
    qkv_shift = jnp.concatenate([head_bias[0], jnp.zeros_like(head_bias[0]), head_bias[1]])
    unit_shift = up_bias.astype(jnp.float32)
    local_rows = inputs.shape[2]
    group_rows = local_rows * groups
    images = group_rows // SEQ
    heads_here = local_width // HEAD_DIM
    row_image = (lax.axis_index("mp") * local_rows + jnp.arange(local_rows, dtype=jnp.int32)) // SEQ
    qkv_total = jnp.zeros((width, 3 * local_width), jnp.float32)
    out_total = jnp.zeros((local_width, width), jnp.float32)
    up_total = jnp.zeros((width, unit_width), jnp.float32)
    down_total = jnp.zeros((unit_width, width), jnp.float32)
    gain_total = jnp.zeros((2, width), jnp.float32)
    shift_total = jnp.zeros((2, width), jnp.float32)
    outb_total = jnp.zeros((2, width), jnp.float32)
    head_total = jnp.zeros((3 * local_width,), jnp.float32)
    unit_total = jnp.zeros((unit_width,), jnp.float32)
    output_list = []
    grad_list = []
    for batch_index in range(inputs.shape[0]):
        live = (row_image < counts[batch_index, 0])[:, None]
        source = inputs[batch_index, 0].astype(jnp.float32)
        first, normed_one, inverse_one = normalize(source, gain_wide[0], shift_wide[0])
        first_low = first.astype(jnp.bfloat16)
        grad_out = jnp.where(live, cotangent[batch_index, 0].astype(jnp.float32), 0.0)
        grad_low = grad_out.astype(jnp.bfloat16)
        gathered_one = lax.all_gather(first_low, "mp", axis=0, tiled=True)
        packed_low = (
            jnp.dot(gathered_one, qkv_matrix, preferred_element_type=jnp.float32) + qkv_shift
        ).astype(jnp.bfloat16)
        blocks = packed_low.reshape(images, SEQ, 3, heads_here, HEAD_DIM)
        mixed, log_total = lax.map(attend, blocks)
        mixed_flat = mixed.reshape(group_rows, local_width)
        attention_term = jnp.dot(mixed_flat, out_full, preferred_element_type=jnp.float32)
        branch = lax.psum_scatter(
            attention_term.astype(jnp.bfloat16), "mp", scatter_dimension=0, tiled=True
        ).astype(jnp.float32)
        middle = source + branch + bias_wide[0]
        second, normed_two, inverse_two = normalize(middle, gain_wide[1], shift_wide[1])
        second_low = second.astype(jnp.bfloat16)
        gathered_two = lax.all_gather(second_low, "mp", axis=0, tiled=True)
        hidden = jnp.dot(gathered_two, up_full, preferred_element_type=jnp.float32) + unit_shift
        act = jax.nn.gelu(hidden, approximate=False).astype(jnp.bfloat16)
        feed_term = jnp.dot(act, down_full, preferred_element_type=jnp.float32)
        feed = lax.psum_scatter(
            feed_term.astype(jnp.bfloat16), "mp", scatter_dimension=0, tiled=True
        ).astype(jnp.float32)
        result = middle + feed + bias_wide[1]
        output_list.append(jnp.where(live, result, 0.0).astype(jnp.bfloat16))
        piece = lax.all_gather(grad_low, "mp", axis=0, tiled=True)
        down_acc = down_total
        down_acc = down_acc + transposed_product(act, piece)
        act_grad = product_by_transpose(piece, down_full)
        down_total, act_grad = (down_acc, act_grad)
        hidden_grad = (act_grad * gelu_slope(hidden)).astype(jnp.bfloat16)
        unit_total = unit_total + jnp.sum(hidden_grad, axis=0, dtype=jnp.float32)
        second_term = product_by_transpose(hidden_grad, up_full)
        second_grad = lax.psum_scatter(
            second_term.astype(jnp.bfloat16), "mp", scatter_dimension=0, tiled=True
        ).astype(jnp.float32)
        up_total = up_total + transposed_product(
            lax.all_gather(second_low, "mp", axis=0, tiled=True), hidden_grad
        )
        middle_grad = grad_out + normalize_back(second_grad, normed_two, inverse_two, gain_wide[1])
        branch_low = middle_grad.astype(jnp.bfloat16)
        mixed_piece = lax.all_gather(branch_low, "mp", axis=0, tiled=True)
        out_acc = out_total
        out_acc = out_acc + transposed_product(mixed_flat, mixed_piece)
        mixed_grad = product_by_transpose(mixed_piece, out_full).astype(jnp.bfloat16)
        out_total, mixed_grad = (out_acc, mixed_grad)
        packed_grad = lax.map(
            attend_back, (blocks, mixed_grad.reshape(images, SEQ, heads_here, HEAD_DIM), log_total)
        )
        packed_grad = packed_grad.reshape(group_rows, 3 * local_width)
        head_total = head_total + jnp.sum(packed_grad, axis=0, dtype=jnp.float32)
        first_term = product_by_transpose(packed_grad, qkv_matrix)
        first_grad = lax.psum_scatter(
            first_term.astype(jnp.bfloat16), "mp", scatter_dimension=0, tiled=True
        ).astype(jnp.float32)
        qkv_total = qkv_total + transposed_product(
            lax.all_gather(first_low, "mp", axis=0, tiled=True), packed_grad
        )
        grad_list.append(
            middle_grad + normalize_back(first_grad, normed_one, inverse_one, gain_wide[0])
        )
        gain_total = gain_total + jnp.stack(
            [jnp.sum(first_grad * normed_one, axis=0), jnp.sum(second_grad * normed_two, axis=0)]
        )
        shift_total = shift_total + jnp.stack(
            [jnp.sum(first_grad, axis=0), jnp.sum(second_grad, axis=0)]
        )
        outb_total = outb_total + jnp.stack(
            [jnp.sum(middle_grad, axis=0), jnp.sum(grad_out, axis=0)]
        )
    (
        qkv_grad,
        out_weight_grad,
        up_weight_grad,
        down_weight_grad,
        gain_part,
        shift_part,
        outb_part,
    ) = (
        lax.psum_scatter(
            qkv_total.reshape(width, 3, local_width).astype(jnp.bfloat16),
            "dp",
            scatter_dimension=0,
            tiled=True,
        ).astype(jnp.float32),
        lax.psum_scatter(
            out_total.astype(jnp.bfloat16), "dp", scatter_dimension=1, tiled=True
        ).astype(jnp.float32),
        lax.psum_scatter(
            up_total.astype(jnp.bfloat16), "dp", scatter_dimension=0, tiled=True
        ).astype(jnp.float32),
        lax.psum_scatter(
            down_total.astype(jnp.bfloat16), "dp", scatter_dimension=1, tiled=True
        ).astype(jnp.float32),
        lax.psum_scatter(
            gain_total.astype(jnp.bfloat16), "dp", scatter_dimension=1, tiled=True
        ).astype(jnp.float32),
        lax.psum_scatter(
            shift_total.astype(jnp.bfloat16), "dp", scatter_dimension=1, tiled=True
        ).astype(jnp.float32),
        lax.psum_scatter(
            outb_total.astype(jnp.bfloat16), "dp", scatter_dimension=1, tiled=True
        ).astype(jnp.float32),
    )
    norm_gain_grad, norm_shift_grad, out_bias_grad = lax.psum(
        (gain_part, shift_part, outb_part), "mp"
    )
    head_sum, up_bias_grad = lax.psum((head_total, unit_total), "dp")
    head_parts = head_sum.reshape(3, local_width)
    qv_bias_grad = jnp.stack([head_parts[0], head_parts[2]])
    outputs = jnp.stack(output_list)[:, None]
    input_grad = jnp.stack(grad_list)[:, None]
    return (
        outputs,
        input_grad,
        qkv_grad,
        qv_bias_grad,
        out_weight_grad,
        up_weight_grad,
        up_bias_grad,
        down_weight_grad,
        norm_gain_grad,
        norm_shift_grad,
        out_bias_grad,
    )


def solution(mesh):
    in_specs = (
        P(None, "dp", "mp", None),
        P(None, "dp", "mp", None),
        P(None, "dp"),
        P("dp", None, "mp"),
        P(None, "mp"),
        P("mp", "dp"),
        P("dp", "mp"),
        P("mp"),
        P("mp", "dp"),
        P(None, "dp"),
        P(None, "dp"),
        P(None, "dp"),
    )
    out_specs = (
        P(None, "dp", "mp", None),
        P(None, "dp", "mp", None),
        P("dp", None, "mp"),
        P(None, "mp"),
        P("mp", "dp"),
        P("dp", "mp"),
        P("mp"),
        P("mp", "dp"),
        P(None, "dp"),
        P(None, "dp"),
        P(None, "dp"),
    )
    return jax.shard_map(shards, mesh=mesh, in_specs=in_specs, out_specs=out_specs, check_vma=False)
```

profile of v0, /device:TPU:0, one launch (start us, length us, event | category | flops | bytes accessed | tf_op | source)
XLA Modules:
  0.0 1697.2 jit_solution(7373851201050650407)
XLA Ops:
  7.2 13.5 all_gather.49
  20.8 8.8 all_gather.50
  58.2 10.1 all_gather.54
  68.3 14.1 all_gather.53
  82.3 16.4 all-gather.26.cloned.1.call-done
  104.5 23.5 %all-gather.20.cloned.1.call-done = bf16[1024,3,256]{0,2,1:T(8,128)(2,1)} async-done(((bf16[128,3,256]{0,2,1:T(8,128)(2,1)}), bf16[1024,3,256]{0,2,1:T(8,128)(2,1)}) %all-gather.20.cloned.1.call-update) | async-done | bytes 1572880 | tf_op jit(solution)/shard_map/all_gather | solution.py:109
  128.1 8.5 add_convert_fusion.1
  136.6 11.4 reshape.260
  148.0 10.4 copy.85
  158.6 20.2 %while.44 = (s32[]{:T(128)}, bf16[4,577,4,64]{1,3,2,0:T(8,128)(2,1)S(1)}, f32[4,4,577]{2,1,0:T(4,128)S(1)}, bf16[4,577,3,4,64]{1,4,3,2,0:T(8,128)(2,1)}, s32[]{:T(128)}) while((s32[]{:T(128)}, bf16[4,577,4,64]{1,3,2,0:T(8,128)(2,1)S(1)}, f32[4,4,577]{2,1,0:T(4,128)S(1)}, bf16[4,577,3,4,64]{1,4,3,2,0:T(8,128)(2,1)}, s32[]{:T(128)}) %tuple.137), condition=%wide.region_5.6_spmd, body=%wide.region_2.5_spmd.sunk | while | flops 353050112 | bytes 19796128 | solution.py:156
  178.8 7.9 all-gather.30.cloned.1.call-done
  192.5 8.7 add_convert_fusion
  201.2 11.0 reshape.261
  212.2 10.6 copy.89
  223.0 20.1 %while.45 = (s32[]{:T(128)}, bf16[4,577,4,64]{1,3,2,0:T(8,128)(2,1)S(1)}, f32[4,4,577]{2,1,0:T(4,128)S(1)}, bf16[4,577,3,4,64]{1,4,3,2,0:T(8,128)(2,1)}, s32[]{:T(128)}) while((s32[]{:T(128)}, bf16[4,577,4,64]{1,3,2,0:T(8,128)(2,1)S(1)}, f32[4,4,577]{2,1,0:T(4,128)S(1)}, bf16[4,577,3,4,64]{1,4,3,2,0:T(8,128)(2,1)}, s32[]{:T(128)}) %tuple.140), condition=%wide.region_15.16_spmd, body=%wide.region_12.15_spmd.sunk | while | flops 353050112 | bytes 19796128 | solution.py:156
  262.7 192.6 %fusion.177 = (bf16[592,1024]{1,0:T(8,128)(2,1)}, bf16[592,1024]{1,0:T(8,128)(2,1)}) fusion(bf16[2308,1024]{1,0:T(8,128)(2,1)} %convolution_convert_fusion.7, bf16[2308,1024]{1,0:T(8,128)(2,1)} %convolution_convert_fusion.5), kind=kCustom, calls=%all-reduce-scatter.10 | all-reduce-scatter fusion | flops 4849665 | bytes 11878912
  465.0 7.5 concatenate.6
  502.1 42.7 %all-gather.28.cloned.1.call-done = bf16[4,577,1024]{2,1,0:T(8,128)(2,1)} async-done(((bf16[1,577,1024]{2,1,0:T(8,128)(2,1)}), bf16[4,577,1024]{2,1,0:T(8,128)(2,1)}) %all-gather.28.cloned.1.call-update) | async-done | bytes 4726800 | tf_op jit(solution)/shard_map/all_gather | solution.py:165
  550.6 53.7 %all-gather.32.cloned.1.call-done = bf16[4,577,1024]{2,1,0:T(8,128)(2,1)} async-done(((bf16[1,577,1024]{2,1,0:T(8,128)(2,1)}), bf16[4,577,1024]{2,1,0:T(8,128)(2,1)}) %all-gather.32.cloned.1.call-update) | async-done | bytes 4726800 | tf_op jit(solution)/shard_map/all_gather | solution.py:165
  610.0 25.0 %all-gather.22.cloned.1.call-done = bf16[1024,1024]{1,0:T(8,128)(2,1)} async-done(((bf16[128,1024]{1,0:T(8,128)(2,1)}), bf16[1024,1024]{1,0:T(8,128)(2,1)}) %all-gather.22.cloned.1.call-update) | async-done | bytes 2097168 | tf_op jit(solution)/shard_map/all_gather | solution.py:111
  635.0 10.5 fusion.190
  645.5 21.4 %all-gather.24.cloned.1.call-done = bf16[1024,1024]{1,0:T(8,128)(2,1)} async-done(((bf16[1024,128]{1,0:T(8,128)(2,1)}), bf16[1024,1024]{1,0:T(8,128)(2,1)}) %all-gather.24.cloned.1.call-update) | async-done | bytes 2097168 | tf_op jit(solution)/shard_map/all_gather | solution.py:112
  666.9 12.4 convert_reduce_fusion
  688.4 49.9 %fusion.74 = (bf16[2308,1024]{1,0:T(8,128)(2,1)}, bf16[2308,1024]{1,0:T(8,128)(2,1)}, f32[2308,1024]{1,0:T(8,128)}) fusion(f32[1024]{0:T(1024)S(1)} %convert_element_type.277, f32[2308,1024]{1,0:T(8,128)S(1)} %bitcast.540, bf16[2308,1024]{1,0:T(8,128)(2,1)} %reshape.227, bf16[1024,1024]{1,0:T(8,128)(2,1)S(1)} %copy-done.85), kind=kOutput, calls=%fused_computation.98 | convolution fusion | flops 5152194560 | bytes 35188736 | tf_op jit(solution)/shard_map/dot_general | solution.py:166
  738.3 11.2 convert_reduce_fusion.1
  758.5 164.8 %fusion.176 = (bf16[592,1024]{1,0:T(8,128)(2,1)}, bf16[592,1024]{1,0:T(8,128)(2,1)}) fusion(bf16[2308,1024]{1,0:T(8,128)(2,1)} %convolution_convert_fusion.3, bf16[2308,1024]{1,0:T(8,128)(2,1)} %convolution_convert_fusion.2), kind=kCustom, calls=%all-reduce-scatter.9 | all-reduce-scatter fusion | flops 4849665 | bytes 11878912
  931.8 7.5 concatenate.10
  964.8 10.8 fusion.194
  976.6 9.8 add_convert_fusion.2
  989.1 9.0 fusion.193
  998.2 9.4 add_convert_fusion.3
  1007.7 9.7 convolution_convert_fusion.4
  1017.4 9.1 convolution_convert_fusion.6
  1044.3 39.7 %while.47 = (s32[]{:T(128)}, bf16[4,577,3,4,64]{1,4,3,2,0:T(8,128)(2,1)}, bf16[4,577,3,4,64]{1,4,3,2,0:T(8,128)(2,1)}, f32[4,4,577]{2,1,0:T(4,128)}, bf16[4,577,4,64]{1,3,2,0:T(8,128)(2,1)S(1)}, /*index=5*/s32[]{:T(128)}) while((s32[]{:T(128)}, bf16[4,577,3,4,64]{1,4,3,2,0:T(8,128)(2,1)}, bf16[4,577,3,4,64]{1,4,3,2,0:T(8,128)(2,1)}, ...), condition=%wide.region_34.35_spmd, body=%wide.region_32.34_spmd.sunk | while | flops 871673856 | bytes 48799992 | solution.py:195
  1091.1 7.8 reshape.221
  1116.5 40.1 %while.46 = (s32[]{:T(128)}, bf16[4,577,3,4,64]{1,4,3,2,0:T(8,128)(2,1)}, bf16[4,577,3,4,64]{1,4,3,2,0:T(8,128)(2,1)}, f32[4,4,577]{2,1,0:T(4,128)}, bf16[4,577,4,64]{1,3,2,0:T(8,128)(2,1)S(1)}, /*index=5*/s32[]{:T(128)}) while((s32[]{:T(128)}, bf16[4,577,3,4,64]{1,4,3,2,0:T(8,128)(2,1)}, bf16[4,577,3,4,64]{1,4,3,2,0:T(8,128)(2,1)}, ...), condition=%wide.region_25.26_spmd, body=%wide.region_23.25_spmd.sunk | while | flops 871673856 | bytes 48799992 | solution.py:195
  1163.7 7.7 reshape.219
  1171.5 7.9 convolution_convert_fusion
  1185.1 321.5 %fusion.175 = (bf16[592,1024]{1,0:T(8,128)(2,1)}, bf16[592,1024]{1,0:T(8,128)(2,1)S(1)}, bf16[592,1024]{1,0:T(8,128)(2,1)S(1)}, bf16[592,1024]{1,0:T(8,128)(2,1)}) fusion(bf16[2308,1024]{1,0:T(8,128)(2,1)} %convolution_convert_fusion.4, bf16[2308,1024]{1,0:T(8,128)(2,1)} %convolution_convert_fusion.6, bf16[2308,1024]{1,0:T(8,128)(2,1)} %convolution_convert_fusion, ...), kind=kCustom, calls=%all-reduce-scatter.8 | all-reduce-scatter fusion | flops 9699329 | bytes 23757312
  1517.3 9.3 fusion.191
  1543.9 7.3 concatenate.5
  1554.2 7.7 fusion.138
  1569.8 8.6 add_convert_fusion.4
  1591.2 14.8 all-reduce.16
  1621.5 9.6 copy.103
  1636.8 8.0 all-reduce.17
  1644.8 8.8 reduce-scatter.38.cloned.1.call-done
  1655.2 33.0 %reduce-scatter.34.cloned.1.call-done = bf16[128,3,256]{2,0,1:T(8,128)(2,1)} async-done(((bf16[1024,3,256]{2,0,1:T(8,128)(2,1)}), bf16[128,3,256]{2,0,1:T(8,128)(2,1)}) %reduce-scatter.34.cloned.1.call-update) | async-done | bytes 196624 | tf_op jit(solution)/shard_map/reduce_scatter | solution.py:228
  (488 shorter events, 415.0 us)
Async XLA Ops:
  7.2 91.5 %all-gather.26.cloned.1.call-start = ((), (), s32[]{:S(2)}) async-start(), calls=%async_computation.12 | async-start | bytes 5980160 | tf_op jit(solution)/shard_map/all_gather | solution.py:151
  41.6 86.5 %all-gather.20.cloned.1.call-start = ((), (), s32[]{:S(2)}) async-start(), calls=%async_computation.7 | async-start | bytes 1769472 | tf_op jit(solution)/shard_map/all_gather | solution.py:109
  42.5 144.3 %all-gather.30.cloned.1.call-start = ((), (), s32[]{:S(2)}) async-start(), calls=%async_computation.14 | async-start | bytes 5980160 | tf_op jit(solution)/shard_map/all_gather | solution.py:151
  43.2 447.0 %all-gather.38.cloned.1.call-start = ((), (), s32[]{:S(2)}) async-start(), calls=%async_computation.18 | async-start | bytes 5980160 | tf_op jit(solution)/shard_map/all_gather | solution.py:174
  54.7 441.2 %all-gather.34.cloned.1.call-start = ((), (), s32[]{:S(2)}) async-start(), calls=%async_computation.16 | async-start | bytes 5980160 | tf_op jit(solution)/shard_map/all_gather | solution.py:174
  58.1 486.7 %all-gather.28.cloned.1.call-start = ((), (), s32[]{:S(2)}) async-start(), calls=%async_computation.13 | async-start | bytes 5980160 | tf_op jit(solution)/shard_map/all_gather | solution.py:165
  82.3 176.8 %copy-start.31 = (bf16[256,1024]{1,0:T(8,128)(2,1)}, bf16[256,1024]{1,0:T(8,128)(2,1)S(1)}, u32[]{:S(2)}) copy-start(bf16[256,1024]{1,0:T(8,128)(2,1)S(1)} %all_gather.53) | copy-start | bytes 1572868
  262.7 200.4 %copy-start.62 = (bf16[2,1024]{1,0:T(2,128)(2,1)S(1)}, bf16[2,1024]{1,0:T(2,128)(2,1)}, u32[]{:S(2)}) copy-start(bf16[2,1024]{1,0:T(2,128)(2,1)} %all_gather.54) | copy-start | bytes 12292
  262.7 201.0 %copy-start.82 = (u32[32]{0:T(128)S(1)}, u32[32]{0:T(128)}, u32[]{:S(2)}) copy-start(u32[32]{0:T(128)} %constant.173) | copy-start | bytes 388
  455.3 24.5 %copy-start.1 = (bf16[1,1,577,1024]{3,2,1,0:T(8,128)(2,1)S(1)}, bf16[1,1,577,1024]{3,2,1,0:T(8,128)(2,1)}, u32[]{:S(2)}) copy-start(bf16[1,1,577,1024]{3,2,1,0:T(8,128)(2,1)} %copy-done) | copy-start | bytes 3545092
  455.3 24.5 %copy-start.5 = (bf16[1,1,577,1024]{3,2,1,0:T(8,128)(2,1)S(1)}, bf16[1,1,577,1024]{3,2,1,0:T(8,128)(2,1)}, u32[]{:S(2)}) copy-start(bf16[1,1,577,1024]{3,2,1,0:T(8,128)(2,1)} %copy-done.4) | copy-start | bytes 3545092
  457.3 7.7 collective-permute-start.2
  458.6 13.9 collective-permute-start
  463.8 20.8 %copy-start.34 = (f32[1,1024]{1,0:T(1,128)}, f32[1,1024]{1,0:T(1,128)S(1)}, u32[]{:S(2)}) copy-start(f32[1,1024]{1,0:T(1,128)S(1)} %get-tuple-element.324) | copy-start | bytes 12292
  487.9 116.4 %all-gather.32.cloned.1.call-start = ((), (), s32[]{:S(2)}) async-start(), calls=%async_computation.15 | async-start | bytes 5980160 | tf_op jit(solution)/shard_map/all_gather | solution.py:165
  488.6 146.3 %all-gather.22.cloned.1.call-start = ((), (), s32[]{:S(2)}) async-start(), calls=%async_computation.8 | async-start | bytes 2359296 | tf_op jit(solution)/shard_map/all_gather | solution.py:111
  489.4 177.5 %all-gather.24.cloned.1.call-start = ((), (), s32[]{:S(2)}) async-start(), calls=%async_computation.9 | async-start | bytes 2359296 | tf_op jit(solution)/shard_map/all_gather | solution.py:112
  490.1 536.4 %all-gather.40.cloned.1.call-start = ((), (), s32[]{:S(2)}) async-start(), calls=%async_computation.19 | async-start | bytes 5980160 | tf_op jit(solution)/shard_map/all_gather | solution.py:190
  645.5 36.0 %copy-start.85 = (bf16[1024,1024]{1,0:T(8,128)(2,1)S(1)}, bf16[1024,1024]{1,0:T(8,128)(2,1)}, u32[]{:S(2)}) copy-start(bf16[1024,1024]{1,0:T(8,128)(2,1)} %all-gather.22.cloned.1.call-done) | copy-start | bytes 6291460
  666.9 21.4 %slice-start.4 = ((s8[9469952]{0:T(1024)(128)(4,1)}), s8[4194304]{0:T(1024)(128)(4,1)S(1)}, s32[]{:S(2)}) async-start(s8[9469952]{0:T(1024)(128)(4,1)} %bitcast.539), calls=%async_computation.29 | async-start | bytes 8388608
  666.9 21.4 %slice-start.5 = ((s8[9469952]{0:T(1024)(128)(4,1)}), s8[4194304]{0:T(1024)(128)(4,1)S(1)}, s32[]{:S(2)}) async-start(s8[9469952]{0:T(1024)(128)(4,1)} %bitcast.539), calls=%async_computation.30 | async-start | bytes 8388608
  688.3 49.9 %copy-start.30 = (bf16[2308,1024]{1,0:T(8,128)(2,1)S(1)}, bf16[2308,1024]{1,0:T(8,128)(2,1)}, u32[]{:S(2)}) copy-start(bf16[2308,1024]{1,0:T(8,128)(2,1)} %reshape.233) | copy-start | bytes 14180356
  688.3 49.9 %copy-start.83 = (bf16[1024,1024]{1,0:T(8,128)(2,1)S(1)}, bf16[1024,1024]{1,0:T(8,128)(2,1)}, u32[]{:S(2)}) copy-start(bf16[1024,1024]{1,0:T(8,128)(2,1)} %all-gather.24.cloned.1.call-done) | copy-start | bytes 6291460
  923.3 23.2 %copy-start.2 = (bf16[1,1,577,1024]{3,2,1,0:T(8,128)(2,1)S(1)}, bf16[1,1,577,1024]{3,2,1,0:T(8,128)(2,1)}, u32[]{:S(2)}) copy-start(bf16[1,1,577,1024]{3,2,1,0:T(8,128)(2,1)} %copy-done) | copy-start | bytes 3545092
  923.3 23.2 %copy-start.6 = (bf16[1,1,577,1024]{3,2,1,0:T(8,128)(2,1)S(1)}, bf16[1,1,577,1024]{3,2,1,0:T(8,128)(2,1)}, u32[]{:S(2)}) copy-start(bf16[1,1,577,1024]{3,2,1,0:T(8,128)(2,1)} %copy-done.4) | copy-start | bytes 3545092
  923.3 23.2 %copy-start.35 = (f32[1,1024]{1,0:T(1,128)S(1)}, f32[1,1024]{1,0:T(1,128)}, u32[]{:S(2)}) copy-start(f32[1,1024]{1,0:T(1,128)} %copy-done.34) | copy-start | bytes 12292
  923.3 23.2 %copy-start.41 = (f32[577]{0:T(1024)S(1)}, f32[577]{0:T(1024)}, u32[]{:S(2)}) copy-start(f32[577]{0:T(1024)} %copy-done.40) | copy-start | bytes 6928
  923.3 23.2 %copy-start.43 = (f32[577]{0:T(1024)S(1)}, f32[577]{0:T(1024)}, u32[]{:S(2)}) copy-start(f32[577]{0:T(1024)} %copy-done.42) | copy-start | bytes 6928
  923.3 23.2 %copy-start.45 = (f32[1,1024]{1,0:T(1,128)S(1)}, f32[1,1024]{1,0:T(1,128)}, u32[]{:S(2)}) copy-start(f32[1,1024]{1,0:T(1,128)} %get-tuple-element.327) | copy-start | bytes 12292
  923.3 23.2 %copy-start.53 = (f32[577]{0:T(1024)S(1)}, f32[577]{0:T(1024)}, u32[]{:S(2)}) copy-start(f32[577]{0:T(1024)} %copy-done.52) | copy-start | bytes 6928
  923.4 23.2 %copy-start.55 = (f32[577]{0:T(1024)S(1)}, f32[577]{0:T(1024)}, u32[]{:S(2)}) copy-start(f32[577]{0:T(1024)} %copy-done.54) | copy-start | bytes 6928
  924.4 7.4 collective-permute-start.6
  928.4 10.8 collective-permute-start.4
  958.3 140.6 %all-gather.36.cloned.1.call-start = ((), (), s32[]{:S(2)}) async-start(), calls=%async_computation.17 | async-start | bytes 5980160 | tf_op jit(solution)/shard_map/all_gather | solution.py:190
  964.8 615.3 %reduce-scatter.46.cloned.1.call-start = ((), (), s32[]{:S(2)}) async-start(), calls=%async_computation.24 | async-start | bytes 294912
  976.6 604.3 %reduce-scatter.40.cloned.1.call-start = ((), (), s32[]{:S(2)}) async-start(), calls=%async_computation.21 | async-start | bytes 2359296
  989.1 593.8 %reduce-scatter.36.cloned.1.call-start = ((), (), s32[]{:S(2)}) async-start(), calls=%async_computation.11 | async-start | bytes 2359296 | tf_op jit(solution)/shard_map/reduce_scatter | solution.py:237
  1007.7 627.4 %reduce-scatter.44.cloned.1.call-start = ((), (), s32[]{:S(2)}) async-start(), calls=%async_computation.23 | async-start | bytes 294912
  1506.6 20.1 %copy-start.26 = (bf16[592,1024]{1,0:T(8,128)(2,1)}, bf16[592,1024]{1,0:T(8,128)(2,1)S(1)}, u32[]{:S(2)}) copy-start(bf16[592,1024]{1,0:T(8,128)(2,1)S(1)} %get-tuple-element.275) | copy-start | bytes 3637252
  1507.9 21.5 %collective-permute-start.5 = (bf16[45,1024]{1,0:T(8,128)(2,1)S(1)}, bf16[45,1024]{1,0:T(8,128)(2,1)S(1)}, u32[]{:S(2)}, u32[]{:S(2)}) collective-permute-start(bf16[45,1024]{1,0:T(8,128)(2,1)S(1)} %slice.143), channel_id=1, source_target_pairs={{0,1},{1,2},{2,3},{4,5},{5,6},{6,7},{8,9},{9,10},{10,11},{12,13},{... | collective-permute-start | bytes 276488
  1510.3 26.3 %collective-permute-start.7 = (bf16[45,1024]{1,0:T(8,128)(2,1)S(1)}, bf16[45,1024]{1,0:T(8,128)(2,1)S(1)}, u32[]{:S(2)}, u32[]{:S(2)}) collective-permute-start(bf16[45,1024]{1,0:T(8,128)(2,1)S(1)} %slice.145), channel_id=1, source_target_pairs={{0,1},{1,2},{2,3},{4,5},{5,6},{6,7},{8,9},{9,10},{10,11},{12,13},{... | collective-permute-start | bytes 276488
  1514.5 29.4 %collective-permute-start.1 = (bf16[45,1024]{1,0:T(8,128)(2,1)S(1)}, bf16[45,1024]{1,0:T(8,128)(2,1)S(1)}, u32[]{:S(2)}, u32[]{:S(2)}) collective-permute-start(bf16[45,1024]{1,0:T(8,128)(2,1)S(1)} %slice.139), channel_id=1, source_target_pairs={{0,1},{1,2},{2,3},{4,5},{5,6},{6,7},{8,9},{9,10},{10,11},{12,13},{... | collective-permute-start | bytes 276488
  1562.8 73.1 %reduce-scatter.42.cloned.1.call-start = ((), (), s32[]{:S(2)}) async-start(), calls=%async_computation.22 | async-start | bytes 294912
  1563.8 89.8 %reduce-scatter.38.cloned.1.call-start = ((), (), s32[]{:S(2)}) async-start(), calls=%async_computation.20 | async-start | bytes 589824
  1569.7 118.5 %reduce-scatter.34.cloned.1.call-start = ((), (), s32[]{:S(2)}) async-start(), calls=%async_computation.10 | async-start | bytes 1769472 | tf_op jit(solution)/shard_map/reduce_scatter | solution.py:228
  1587.6 26.2 %copy-start.13 = (bf16[637,1024]{1,0:T(8,128)(2,1)S(1)}, bf16[637,1024]{1,0:T(8,128)(2,1)}, u32[]{:S(2)}) copy-start(bf16[637,1024]{1,0:T(8,128)(2,1)} %concatenate.6) | copy-start | bytes 3913732
  1587.6 26.2 %copy-start.72 = (pred[577]{0:T(1024)(128)(4,1)S(1)}, pred[577]{0:T(1024)(128)(4,1)}, u32[]{:S(2)}) copy-start(pred[577]{0:T(1024)(128)(4,1)} %copy-done.70) | copy-start | bytes 1735
  1589.3 17.2 %collective-permute-start.3 = (bf16[45,1024]{1,0:T(8,128)(2,1)S(1)}, bf16[45,1024]{1,0:T(8,128)(2,1)S(1)}, u32[]{:S(2)}, u32[]{:S(2)}) collective-permute-start(bf16[45,1024]{1,0:T(8,128)(2,1)S(1)} %slice.141), channel_id=1, source_target_pairs={{0,1},{1,2},{2,3},{4,5},{5,6},{6,7},{8,9},{9,10},{10,11},{12,13},{... | collective-permute-start | bytes 276488
  (74 other events, 526.5 us)
Sparse Core Ops, SparseCore 0:
  41.7 56.9 all-gather.25
  100.9 27.1 all-gather.19
  129.9 56.7 all-gather.29
  188.4 57.6 all-gather.37
  247.7 85.2 all-gather.33
  488.0 56.7 all-gather.27
  546.6 57.6 all-gather.31
  605.8 29.0 all-gather.21
  636.6 30.3 all-gather.23
  958.5 56.6 all-gather.39
  1017.0 57.6 all-gather.35
  1077.3 30.3 reduce-scatter.45
  1110.1 33.9 reduce-scatter.39
  1146.4 34.2 reduce-scatter.35
  1562.9 28.0 reduce-scatter.43
  1593.7 28.5 reduce-scatter.41
  1624.5 29.0 reduce-scatter.37
  1655.7 32.4 reduce-scatter.33
where the time goes:
time: 1710 us; the launch traced here: 1700 us
  blocking collectives  748 us (44%)
  local copies, waits for them, and re-layouts  292 us (17%)
  matrix products  291 us (17%)
  waiting for transfers between devices  235 us (14%)
  other arithmetic  88.5 us (5%)
  starting transfers between devices  24.7 us (1%)
    unnamed x3, blocking collectives  679 us
    unnamed x230, local copies, waits for them, and re-layouts  147 us
    all_gather x2, waiting for transfers between devices, shards(): gathered_two = lax.all_gather(second_low, 'mp', axis=0, tiled=True)  96.3 us
    dot_general x8, matrix products, transposed_product(): lax.dot_general(left, right, (((0,), (0,)), ((), ())), preferred_element_...  64.3 us
    dot_general x2, matrix products, shards(): jnp.dot(gathered_two, up_full, preferred_element_type=jnp.float32)  60.4 us
    dot_general x8, matrix products, product_by_transpose(): lax.dot_general(left, right, (((1,), (1,)), ((), ())), preferred_element_...  58.5 us
  transfers between devices with their start and end apart: 26, of which 9 were waited for; matrix products, arithmetic and copies ran while one was open for 62% of the time, Pallas kernels for 0%

commit v1 on v0

v1 whole, which is shorter than its diff:
```python
import jax
import jax.numpy as jnp
from jax import lax
from jax.experimental import pallas as pl
from jax.experimental.pallas import tpu as pltpu
from jax.sharding import PartitionSpec as P

HEAD_DIM = 64
PAIR = 128


norm_eps = 1e-06
half_root = 0.7071067811865476
density_scale = 0.3989422804014327


def transposed_product(left, right):
    return lax.dot_general(
        left, right, (((0,), (0,)), ((), ())), preferred_element_type=jnp.float32
    )


def product_by_transpose(left, right):
    return lax.dot_general(
        left, right, (((1,), (1,)), ((), ())), preferred_element_type=jnp.float32
    )


def normalize(values, gain, shift):
    center = jnp.mean(values, axis=-1, keepdims=True)
    centered = values - center
    spread = jnp.mean(centered * centered, axis=-1, keepdims=True)
    inverse = lax.rsqrt(spread + norm_eps)
    normed = centered * inverse
    return (normed * gain + shift, normed, inverse)


def normalize_back(grad_result, normed, inverse, gain):
    scaled = grad_result * gain
    first_mean = jnp.mean(scaled, axis=-1, keepdims=True)
    second_mean = jnp.mean(scaled * normed, axis=-1, keepdims=True)
    return inverse * (scaled - first_mean - normed * second_mean)


def gelu_slope(values):
    return 0.5 * (1.0 + lax.erf(values * half_root)) + values * density_scale * jnp.exp(
        -0.5 * values * values
    )


def head_masks(rows):
    lane = lax.broadcasted_iota(jnp.int32, (rows, PAIR), 1)
    return (lane < HEAD_DIM, lane >= HEAD_DIM)


def attend_kernel(query_ref, key_ref, value_ref, mixed_ref, log_ref):
    query = query_ref[0] * jnp.bfloat16(HEAD_DIM**-0.5)
    key_block = key_ref[0]
    value = value_ref[0]
    masks = head_masks(query.shape[0])
    parts = []
    for head in range(2):
        own = jnp.where(masks[head], query, jnp.zeros_like(query))
        scores = product_by_transpose(key_block, own)
        top_score = jnp.max(scores, axis=0, keepdims=True)
        weights = jnp.exp(scores - top_score)
        totals = jnp.sum(weights, axis=0, keepdims=True)
        weights_low = (weights * (1.0 / totals)).astype(jnp.bfloat16)
        parts.append(transposed_product(weights_low, value))
        log_ref[0, 0, head : head + 1, :] = top_score + jnp.log(totals)
    mixed_ref[0] = jnp.where(masks[0], parts[0], parts[1]).astype(jnp.bfloat16)


def attend_back_kernel(
    query_ref, key_ref, value_ref, mixed_grad_ref, log_ref, query_out, key_out, value_out
):
    scale = HEAD_DIM**-0.5
    query = query_ref[0] * jnp.bfloat16(scale)
    key_block = key_ref[0]
    value = value_ref[0]
    mixed_grad = mixed_grad_ref[0]
    masks = head_masks(query.shape[0])
    query_parts, key_parts, value_parts = [], [], []
    for head in range(2):
        own = jnp.where(masks[head], query, jnp.zeros_like(query))
        own_grad = jnp.where(masks[head], mixed_grad, jnp.zeros_like(mixed_grad))
        scores = product_by_transpose(key_block, own)
        weights = jnp.exp(scores - log_ref[0, 0, head : head + 1, :])
        weight_grad = product_by_transpose(value, own_grad)
        value_parts.append(
            jnp.dot(weights.astype(jnp.bfloat16), own_grad, preferred_element_type=jnp.float32)
        )
        centre = jnp.sum(weights * weight_grad, axis=0, keepdims=True)
        score_grad = (weights * (weight_grad - centre)).astype(jnp.bfloat16)
        query_parts.append(transposed_product(score_grad, key_block))
        key_parts.append(jnp.dot(score_grad, own, preferred_element_type=jnp.float32))
    query_out[0] = (jnp.where(masks[0], *query_parts) * scale).astype(jnp.bfloat16)
    key_out[0] = (key_parts[0] + key_parts[1]).astype(jnp.bfloat16)
    value_out[0] = (value_parts[0] + value_parts[1]).astype(jnp.bfloat16)


def part_specs(rows, pairs):
    return [
        pl.BlockSpec((1, rows, PAIR), lambda b, h, c=c: (b, 0, c * pairs + h)) for c in range(3)
    ]


def attend(packed):
    images, rows, width3 = packed.shape
    pairs = width3 // (3 * PAIR)
    plain = pl.BlockSpec((1, rows, PAIR), lambda b, h: (b, 0, h))
    logs = pl.BlockSpec((1, 1, 2, rows), lambda b, h: (b, h, 0, 0))
    return pl.pallas_call(
        attend_kernel,
        grid=(images, pairs),
        in_specs=part_specs(rows, pairs),
        out_specs=[plain, logs],
        out_shape=[
            jax.ShapeDtypeStruct((images, rows, width3 // 3), jnp.bfloat16),
            jax.ShapeDtypeStruct((images, pairs, 2, rows), jnp.float32),
        ],
        compiler_params=pltpu.CompilerParams(vmem_limit_bytes=40 * 2**20),
        cost_estimate=pl.CostEstimate(
            flops=images * rows * rows * width3 * 8 // 3,
            bytes_accessed=images * rows * width3 * 3,
            transcendentals=images * pairs * 2 * rows * rows,
        ),
    )(packed, packed, packed)


def attend_back(packed, mixed_grad, logs_in):
    images, rows, width3 = packed.shape
    pairs = width3 // (3 * PAIR)
    plain = pl.BlockSpec((1, rows, PAIR), lambda b, h: (b, 0, h))
    logs = pl.BlockSpec((1, 1, 2, rows), lambda b, h: (b, h, 0, 0))
    return pl.pallas_call(
        attend_back_kernel,
        grid=(images, pairs),
        in_specs=part_specs(rows, pairs) + [plain, logs],
        out_specs=[plain] * 3,
        out_shape=[jax.ShapeDtypeStruct((images, rows, width3 // 3), jnp.bfloat16)] * 3,
        compiler_params=pltpu.CompilerParams(vmem_limit_bytes=48 * 2**20),
        cost_estimate=pl.CostEstimate(
            flops=images * rows * rows * width3 * 20 // 3,
            bytes_accessed=images * rows * width3 * 5,
            transcendentals=images * pairs * 2 * rows * rows,
        ),
    )(packed, packed, packed, mixed_grad, logs_in)


BOTH = ("dp", "mp")


def mm(left, right):
    return jnp.einsum("bsk,kn->bsn", left, right, preferred_element_type=jnp.float32)


def mmt(left, right):
    return jnp.einsum("bsn,kn->bsk", left, right, preferred_element_type=jnp.float32)


def gram(left, right):
    return jnp.einsum("bsk,bsn->kn", left, right, preferred_element_type=jnp.float32)


def column_sum(values):
    return jnp.sum(values, axis=(0, 1), dtype=jnp.float32)


def shards(
    inputs,
    cotangent,
    counts,
    qkv_weight,
    qv_bias,
    out_weight,
    up_weight,
    up_bias,
    down_weight,
    norm_gain,
    norm_shift,
    out_bias,
):
    dps, mps = lax.axis_size("dp"), lax.axis_size("mp")
    rows_dp, local_width = qkv_weight.shape[0], qkv_weight.shape[2]
    width = rows_dp * dps
    units_mp = up_weight.shape[1]
    units = units_mp * mps
    columns_dp = out_weight.shape[1]

    small = jnp.concatenate(
        [norm_gain.reshape(-1), norm_shift.reshape(-1), out_bias.reshape(-1)]
        + [qv_bias.reshape(-1), up_bias]
    )
    small_all = lax.all_gather(small, BOTH, axis=0, tiled=False).reshape(dps, mps, -1)
    qkv_all = lax.all_gather(qkv_weight, BOTH, axis=0, tiled=False)
    out_all = lax.all_gather(out_weight, BOTH, axis=0, tiled=False)
    up_all = lax.all_gather(up_weight, BOTH, axis=0, tiled=False)
    down_all = lax.all_gather(down_weight, BOTH, axis=0, tiled=False)

    split = 6 * columns_dp
    by_dp = small_all[:, 0, :split].reshape(dps, 6, columns_dp)
    by_dp = by_dp.transpose(1, 0, 2).reshape(6, width).astype(jnp.float32)
    gain_wide, shift_wide, bias_wide = by_dp[0:2], by_dp[2:4], by_dp[4:6]
    by_mp = small_all[0, :, split:].astype(jnp.float32)
    head_bias = by_mp[:, : 2 * local_width].reshape(mps, 2, local_width)
    head_bias = head_bias.transpose(1, 0, 2).reshape(2, width)
    unit_shift = by_mp[:, 2 * local_width :].reshape(units)
    qkv_shift = jnp.concatenate([head_bias[0], jnp.zeros_like(head_bias[0]), head_bias[1]])

    qkv_matrix = (
        qkv_all.reshape(dps, mps, rows_dp, 3, local_width)
        .transpose(0, 2, 3, 1, 4)
        .reshape(width, 3 * width)
    )
    out_full = (
        out_all.reshape(dps, mps, local_width, columns_dp)
        .transpose(1, 2, 0, 3)
        .reshape(width, width)
    )
    up_full = (
        up_all.reshape(dps, mps, rows_dp, units_mp).transpose(0, 2, 1, 3).reshape(width, units)
    )
    down_full = (
        down_all.reshape(dps, mps, units_mp, columns_dp)
        .transpose(1, 2, 0, 3)
        .reshape(units, width)
    )

    live = (lax.axis_index("mp") < counts)[:, :, None]
    source = inputs[:, 0].astype(jnp.float32)
    first, normed_one, inverse_one = normalize(source, gain_wide[0], shift_wide[0])
    first_low = first.astype(jnp.bfloat16)
    grad_low = jnp.where(live, cotangent[:, 0], jnp.zeros_like(cotangent[:, 0]))
    grad_out = grad_low.astype(jnp.float32)

    packed = (mm(first_low, qkv_matrix) + qkv_shift).astype(jnp.bfloat16)
    mixed, logs = attend(packed)
    middle = source + mm(mixed, out_full) + bias_wide[0]
    second, normed_two, inverse_two = normalize(middle, gain_wide[1], shift_wide[1])
    second_low = second.astype(jnp.bfloat16)
    hidden = mm(second_low, up_full) + unit_shift
    act = jax.nn.gelu(hidden, approximate=False).astype(jnp.bfloat16)

    down_part = (
        gram(act, grad_low)
        .astype(jnp.bfloat16)
        .reshape(mps, units_mp, dps, columns_dp)
        .transpose(2, 0, 1, 3)
        .reshape(dps * mps, units_mp, columns_dp)
    )
    down_weight_grad = lax.psum_scatter(down_part, BOTH, scatter_dimension=0, tiled=False)

    result = middle + mm(act, down_full) + bias_wide[1]
    outputs = jnp.where(live, result, 0.0).astype(jnp.bfloat16)

    act_grad = mmt(grad_low, down_full)
    hidden_grad = (act_grad * gelu_slope(hidden)).astype(jnp.bfloat16)
    up_part = (
        gram(second_low, hidden_grad)
        .astype(jnp.bfloat16)
        .reshape(dps, rows_dp, mps, units_mp)
        .transpose(0, 2, 1, 3)
        .reshape(dps * mps, rows_dp, units_mp)
    )
    up_weight_grad = lax.psum_scatter(up_part, BOTH, scatter_dimension=0, tiled=False)

    second_grad = mmt(hidden_grad, up_full)
    middle_grad = grad_out + normalize_back(second_grad, normed_two, inverse_two, gain_wide[1])
    branch_low = middle_grad.astype(jnp.bfloat16)
    out_part = (
        gram(mixed, branch_low)
        .astype(jnp.bfloat16)
        .reshape(mps, local_width, dps, columns_dp)
        .transpose(2, 0, 1, 3)
        .reshape(dps * mps, local_width, columns_dp)
    )
    out_weight_grad = lax.psum_scatter(out_part, BOTH, scatter_dimension=0, tiled=False)

    mixed_grad = mmt(branch_low, out_full).astype(jnp.bfloat16)
    grads = attend_back(packed, mixed_grad, logs)
    packed_grad = jnp.concatenate(grads, axis=2)
    qkv_part = (
        gram(first_low, packed_grad)
        .astype(jnp.bfloat16)
        .reshape(dps, rows_dp, 3, mps, local_width)
        .transpose(0, 3, 1, 2, 4)
        .reshape(dps * mps, rows_dp, 3, local_width)
    )
    qkv_grad = lax.psum_scatter(qkv_part, BOTH, scatter_dimension=0, tiled=False)
    first_grad = mmt(packed_grad, qkv_matrix)
    input_grad = middle_grad + normalize_back(first_grad, normed_one, inverse_one, gain_wide[0])

    sums = jnp.concatenate(
        [
            column_sum(first_grad * normed_one),
            column_sum(second_grad * normed_two),
            column_sum(first_grad),
            column_sum(second_grad),
            column_sum(middle_grad),
            column_sum(grad_out),
            column_sum(grads[0]),
            column_sum(grads[2]),
            column_sum(hidden_grad),
        ]
    )
    sums = lax.psum(sums, BOTH)
    six = sums[: 6 * width].reshape(6, width)
    six = lax.dynamic_slice_in_dim(six, lax.axis_index("dp") * columns_dp, columns_dp, 1)
    two = sums[6 * width : 8 * width].reshape(2, width)
    mp_index = lax.axis_index("mp")
    qv_bias_grad = lax.dynamic_slice_in_dim(two, mp_index * local_width, local_width, 1)
    up_bias_grad = lax.dynamic_slice_in_dim(sums[8 * width :], mp_index * units_mp, units_mp, 0)
    wide = jnp.float32
    return (
        outputs[:, None],
        input_grad[:, None],
        qkv_grad.astype(wide),
        qv_bias_grad,
        out_weight_grad.astype(wide),
        up_weight_grad.astype(wide),
        up_bias_grad,
        down_weight_grad.astype(wide),
        six[0:2],
        six[2:4],
        six[4:6],
    )


def solution(mesh):
    in_specs = (
        P(None, "dp", "mp", None),
        P(None, "dp", "mp", None),
        P(None, "dp"),
        P("dp", None, "mp"),
        P(None, "mp"),
        P("mp", "dp"),
        P("dp", "mp"),
        P("mp"),
        P("mp", "dp"),
        P(None, "dp"),
        P(None, "dp"),
        P(None, "dp"),
    )
    out_specs = (
        P(None, "dp", "mp", None),
        P(None, "dp", "mp", None),
        P("dp", None, "mp"),
        P(None, "mp"),
        P("mp", "dp"),
        P("dp", "mp"),
        P("mp"),
        P("mp", "dp"),
        P(None, "dp"),
        P(None, "dp"),
        P(None, "dp"),
    )
    return jax.shard_map(shards, mesh=mesh, in_specs=in_specs, out_specs=out_specs, check_vma=False)
```

time: 1710 us -> 1050 us (0.61)
  blocking collectives: 748 us -> 113 us
  waiting for transfers between devices: 235 us -> 389 us
  matrix products: 291 us -> 172 us
  local copies, waits for them, and re-layouts: 292 us -> 184 us
  Pallas kernels: 0 us -> 91.8 us
  starting transfers between devices: 24.7 us -> 0.32 us
    unnamed x3 -> x0, blocking collectives: 679 us -> none
    reduce_scatter x2 -> x4, waiting for transfers between devices: 33 us -> 289 us  [the longest x1 185 us: shards(): lax.psum_scatter(down_part, BOTH, scatter_dimension=0, tiled=False)]
    dot_general x80 -> x12, matrix products: 291 us -> 172 us  [the longest x4 64.2 us: mmt(): jnp.einsum('bsn,kn->bsk', left, right, preferred_element_type=jnp.float32)]
    unnamed x230 -> x84, local copies, waits for them, and re-layouts: 147 us -> 36.8 us
    all_gather x11 -> x4, waiting for transfers between devices: 191 us -> 97.4 us  [the longest x1 52.4 us: shards(): down_all = lax.all_gather(down_weight, BOTH, axis=0, tiled=False)]
    pallas_call x0 -> x2, Pallas kernels: none -> 91.8 us  [the longest x1 59.4 us: attend_back(): pl.pallas_call(attend_back_kernel, grid=(images, pairs), in_specs=part_sp...]
    reshape x8 -> x12, local copies, waits for them, and re-layouts: 48.1 us -> 110 us  [the longest x2 26.5 us: shards(): up_all.reshape(dps, mps, rows_dp, units_mp).transpose(0, 2, 1, 3)]
    while x8 -> x0, local copies, waits for them, and re-layouts: 47.4 us -> none  [the longest x4 26.9 us: shards(): mixed, log_total = lax.map(attend, blocks)]
  transfers between devices with their start and end apart: 26 -> 8, of which waited for: 9 -> 5; matrix products, arithmetic and copies ran while one was open for 62% -> 30% of each run, Pallas kernels for 0% -> 9%
where the time goes in v1:
time: 1050 us; the launch traced here: 1040 us
  waiting for transfers between devices  389 us (37%)
  local copies, waits for them, and re-layouts  184 us (18%)
  matrix products  172 us (16%)
  blocking collectives  113 us (11%)
  Pallas kernels  91.8 us (9%)
  other arithmetic  74 us (7%)
  between operations  15.1 us (1%)
    reduce_scatter x1, waiting for transfers between devices, shards(): lax.psum_scatter(down_part, BOTH, scatter_dimension=0, tiled=False)  185 us
    reduce_scatter x1, waiting for transfers between devices, shards(): lax.psum_scatter(up_part, BOTH, scatter_dimension=0, tiled=False)  104 us
    all_gather x1, blocking collectives, shards(): lax.all_gather(small, BOTH, axis=0, tiled=False).reshape(dps, mps, -1)  71.6 us
    dot_general x4, matrix products, mmt(): jnp.einsum('bsn,kn->bsk', left, right, preferred_element_type=jnp.float32)  64.2 us
    pallas_call x1, Pallas kernels, attend_back(): pl.pallas_call(attend_back_kernel, grid=(images, pairs), in_specs=part_sp...  59.4 us
    dot_general x4, matrix products, mm(): jnp.einsum('bsk,kn->bsn', left, right, preferred_element_type=jnp.float32)  58.8 us
    all_gather x1, waiting for transfers between devices, shards(): down_all = lax.all_gather(down_weight, BOTH, axis=0, tiled=False)  52.4 us
    dot_general x4, matrix products, gram(): jnp.einsum('bsk,bsn->kn', left, right, preferred_element_type=jnp.float32)  48.8 us
  transfers between devices with their start and end apart: 8, of which 5 were waited for; matrix products, arithmetic and copies ran while one was open for 30% of the time, Pallas kernels for 9%

profile of v1, /device:TPU:0, one launch (start us, length us, event | category | flops | bytes accessed | tf_op | source)
XLA Modules:
  0.0 1039.5 jit_solution(10928723935749448980)
XLA Ops:
  14.3 71.6 %all-gather.5 = bf16[32,1,2304]{2,1,0:T(2,128)(2,1)S(1)} all-gather(bf16[1,1,2304]{2,1,0:T(2,128)(2,1)S(1)} %reshape.227), channel_id=2, replica_groups=mesh['dp'=8,'mp'=4] {'dp','mp'}, dimensions={0}, use_global_device_ids=true | all-gather | bytes 152064 | tf_op jit(solution)/shard_map/all_gather | solution.py:195
  87.8 2.4 convert_reduce_fusion.1
  91.7 3.4 fusion.52
  95.1 4.3 copy.120
  99.4 4.4 reshape.231
  103.8 37.8 %all-gather.11.cloned.1.call-done = bf16[4096,3,256]{2,0,1:T(8,128)(2,1)} async-done(((bf16[128,3,256]{2,0,1:T(8,128)(2,1)}), bf16[4096,3,256]{2,0,1:T(8,128)(2,1)}) %all-gather.11.cloned.1.call-update) | async-done | bytes 6291472 | tf_op jit(solution)/shard_map/all_gather | solution.py:196
  141.6 10.3 copy.119
  151.9 11.7 %reshape.230 = bf16[1024,3072,1]{1,0,2:T(8,128)(2,1)} reshape(bf16[8,128,3,4,256]{4,3,2,1,0:T(4,128)(2,1)} %bitcast.184) | data formatting | bytes 12582912 | tf_op jit(solution)/shard_map/reshape | solution.py:214
  163.6 11.4 %add_convert_fusion.query_ref.key_ref.value_ref = bf16[2,577,3072]{2,1,0:T(8,128)(2,1)S(1)} fusion(f32[3072]{0:T(1024)S(1)} %pad_maximum_fusion, bf16[1024,3072,1]{1,0,2:T(8,128)(2,1)} %reshape.230, f32[1024]{0:T(1024)S(1)} %get-tuple-element.82, f32[1024]{0:T(1024)S(1)} %get-tuple-element.83, f32[2,577]{1,0:T(2,128)S(1)} %add_rsqrt_fusion.1, ...), kind=kOutput, calls=%fused_computation.31 | convolution fusion | flops 7274520576 | bytes 15774736 | tf_op jit(solution)/shard_map/bsk,kn->bsn/dot_general | solution.py:155
  175.1 32.4 %shard_map.203 = (bf16[2,577,1024]{2,1,0:T(8,128)(2,1)S(1)}, f32[2,8,2,577]{3,2,1,0:T(2,128)S(1)}) custom-call(bf16[2,577,3072]{2,1,0:T(8,128)(2,1)S(1)} %add_convert_fusion.query_ref.key_ref.value_ref, bf16[2,577,3072]{2,1,0:T(8,128)(2,1)S(1)} %add_convert_fusion.query_ref.key_ref.value_ref, ...), custom_call_target="tpu_custom_call" | custom-call | flops 5454708736 | bytes 10635264 | tf_op jit(solution)/shard_map/pallas_call | solution.py:113
  207.5 3.5 fusion.63
  211.0 2.2 copy-done.5
  213.8 7.1 all-gather.15.cloned.1.call-done
  221.0 12.1 %copy.118 = bf16[8,4,128,1024]{3,1,2,0:T(4,128)(2,1)} copy(bf16[8,4,128,1024]{3,2,1,0:T(8,128)(2,1)} %bitcast.188) | data formatting | bytes 16777216 | tf_op jit(solution)/shard_map/reshape | solution.py:222
  233.1 14.4 %reshape.232 = bf16[1024,4096,1]{1,0,2:T(8,128)(2,1)} reshape(bf16[8,128,4,1024]{3,2,1,0:T(4,128)(2,1)} %bitcast.179) | data formatting | bytes 16777216 | tf_op jit(solution)/shard_map/reshape | solution.py:222
  247.5 52.4 %all-gather.17.cloned.1.call-done = bf16[32768,128]{1,0:T(8,128)(2,1)} async-done(((bf16[1024,128]{1,0:T(8,128)(2,1)}), bf16[32768,128]{1,0:T(8,128)(2,1)}) %all-gather.17.cloned.1.call-update) | async-done | bytes 8388624 | tf_op jit(solution)/shard_map/all_gather | solution.py:199
  299.9 12.1 %copy.117 = bf16[8,4,1024,128]{3,0,2,1:T(8,128)(2,1)} copy(bf16[8,4,1024,128]{3,2,1,0:T(8,128)(2,1)} %bitcast.189) | data formatting | bytes 16777216 | tf_op jit(solution)/shard_map/reshape | solution.py:225
  312.0 13.4 %reshape.233 = bf16[4096,1024,1]{1,0,2:T(8,128)(2,1)} reshape(bf16[4,1024,8,128]{3,2,1,0:T(8,128)(2,1)} %bitcast.180) | data formatting | bytes 16777216 | tf_op jit(solution)/shard_map/reshape | solution.py:227
  325.4 28.0 %fusion.38 = (u8[577,4096]{1,0:T(8,128)(4,1)}, u8[577,4096]{1,0:T(8,128)(4,1)}, f32[2,577,4096]{2,1,0:T(8,128)}) fusion(f32[4096]{0:T(1024)S(1)} %bitcast.195, bf16[1024,4096,1]{1,0,2:T(8,128)(2,1)} %reshape.232, f32[2,577,1024]{2,1,0:T(8,128)} %copy-done.5, f32[1024]{0:T(1024)S(1)} %get-tuple-element.80, f32[1024]{0:T(1024)S(1)} %get-tuple-element.78, ...), kind=kOutput, calls=%fused_computation.73 | convolution fusion | flops 9747810304 | bytes 36783120 | tf_op jit(solution)/shard_map/bsk,kn->bsn/dot_general | solution.py:155
  353.4 23.1 %convert_reduce_fusion = (f32[4096]{0:T(1024)}, bf16[2,577,4096]{2,1,0:T(8,128)(2,1)}) fusion(f32[2,577,4096]{2,1,0:T(8,128)} %get-tuple-element.95, f32[4096]{0:T(1024)S(1)} %bitcast.196, bf16[4096,1024,1]{1,0,2:T(8,128)(2,1)} %reshape.233, bf16[2,577,1024]{2,0,1:T(2,128)(2,1)} %fusion.52), kind=kOutput, calls=%fused_computation.15 | convolution fusion | flops 9741897728 | bytes 39145472 | tf_op jit(solution)/shard_map/bsn,kn->bsk/dot_general | solution.py:159
  376.4 18.3 %multiply_reduce_fusion = (f32[1024]{0:T(1024)S(1)}, f32[2,577]{1,0:T(2,128)S(1)}, f32[2,577]{1,0:T(2,128)S(1)}, f32[1024]{0:T(1024)S(1)}, f32[2,577,1024]{2,1,0:T(8,128)}) fusion(f32[2,577,1024]{2,1,0:T(8,128)} %copy-done.5, f32[2,577]{1,0:T(2,128)S(1)} %add_rsqrt_fusion, f32[2,577]{1,0:T(2,128)S(1)} %broadcast_multiply_fusion.4, ...), kind=kOutput, calls=%fused_computation.67 | convolution fusion | flops 9691084800 | bytes 27326496 | tf_op jit(solution)/shard_map/bsn,kn->bsk/dot_general | solution.py:159
  394.8 5.1 fusion.60
  399.9 3.2 fusion.53
  403.9 1.8 copy.73
  405.8 6.8 convolution_convert_fusion.mixed_grad_ref
  412.5 59.4 %shard_map.204 = (bf16[2,577,1024]{2,1,0:T(8,128)(2,1)S(1)}, bf16[2,577,1024]{2,1,0:T(8,128)(2,1)S(1)}, bf16[2,577,1024]{2,1,0:T(8,128)(2,1)}) custom-call(bf16[2,577,3072]{2,1,0:T(8,128)(2,1)} %copy-done, bf16[2,577,3072]{2,1,0:T(8,128)(2,1)} %copy-done, bf16[2,577,3072]{2,1,0:T(8,128)(2,1)} %copy-done, ...), custom_call_target="tpu_custom_call" | custom-call | flops 13636771840 | bytes 17725440 | tf_op jit(solution)/shard_map/pallas_call | solution.py:136
  473.9 2.9 copy-done.15
  476.8 12.8 %bitcast_convert_fusion.2 = bf16[1024,3072]{1,0:T(8,128)(2,1)} fusion(bf16[2,577,3072]{2,1,0:T(8,128)(2,1)S(1)} %constant_dynamic-update-slice_fusion, f32[1024]{0:T(1024)S(1)} %copy-done.26, f32[1024]{0:T(1024)S(1)} %copy-done.22, f32[2,577]{1,0:T(2,128)S(1)} %copy-done.20, f32[2,577]{1,0:T(2,128)S(1)} %copy-done.18, ...), kind=kOutput, calls=%fused_computation.32 | convolution fusion | flops 7270576128 | bytes 15762448 | tf_op jit(solution)/shard_map/bsk,bsn->kn/dot_general | solution.py:163
  489.6 12.2 %reshape.203 = bf16[8,128,3,4,256]{4,3,2,1,0:T(4,128)(2,1)} reshape(bf16[1024,3072]{1,0:T(8,128)(2,1)} %bitcast_convert_fusion.2) | data formatting | bytes 12582912 | tf_op jit(solution)/shard_map/reshape | solution.py:286
  501.8 6.8 copy.72
  508.7 18.3 %bitcast_convert_fusion.1 = bf16[1024,4096]{1,0:T(8,128)(2,1)} fusion(bf16[2,577,4096]{2,1,0:T(8,128)(2,1)} %get-tuple-element.94, f32[2,577,1024]{2,1,0:T(8,128)} %copy-done.5, f32[1024]{0:T(1024)S(1)} %get-tuple-element.80, f32[1024]{0:T(1024)S(1)} %get-tuple-element.78, f32[2,577]{1,0:T(2,128)S(1)} %add_rsqrt_fusion, ...), kind=kOutput, calls=%fused_computation.30 | convolution fusion | flops 9690556416 | bytes 22586384 | tf_op jit(solution)/shard_map/bsk,bsn->kn/dot_general | solution.py:163
  527.0 14.6 %reshape.207 = bf16[8,128,4,1024]{3,2,1,0:T(4,128)(2,1)} reshape(bf16[1024,4096]{1,0:T(8,128)(2,1)} %bitcast_convert_fusion.1) | data formatting | bytes 16777216 | tf_op jit(solution)/shard_map/reshape | solution.py:262
  541.6 9.8 copy.74
  551.4 47.2 %fusion.2 = bf16[2,577,4096]{2,1,0:T(8,128)(2,1)S(1)} fusion(f32[2,577,4096]{2,1,0:T(8,128)} %get-tuple-element.95, f32[4096]{0:T(1024)S(1)} %bitcast.197, u8[577,4096]{1,0:T(8,128)(4,1)} %get-tuple-element.66, u8[577,4096]{1,0:T(8,128)(4,1)} %get-tuple-element.65), kind=kLoop, calls=%fused_computation.4 | loop fusion | flops 335601664 | bytes 33103872 | tf_op jit(solution)/shard_map/convert_element_type | solution.py:243
  598.7 3.7 copy-done.9
  602.4 14.5 %fusion.22 = bf16[512,8,8,128]{3,1,2,0:T(8,128)(2,1)} fusion(bf16[2,577,4096]{2,1,0:T(8,128)(2,1)S(1)} %fusion.2, bf16[2,1,577,1024]{3,0,2,1:T(2,128)(2,1)S(1)} %copy-done.12, pred[2]{0:T(512)(128)(4,1)S(1)} %copy-done.28), kind=kOutput, calls=%fused_computation.50 | convolution fusion | flops 9685829632 | bytes 20205570 | tf_op jit(solution)/shard_map/bsk,bsn->kn/dot_general | solution.py:163
  616.9 8.9 copy.83
  625.8 7.3 bitcast_bitcast_fusion
  633.1 8.7 copy.75
  641.9 16.0 %fusion.30 = (f32[1024]{0:T(1024)S(1)}, f32[2,577]{1,0:T(2,128)S(1)}, f32[2,577]{1,0:T(2,128)S(1)}, f32[1024]{0:T(1024)S(1)}, f32[2,577,1024]{2,1,0:T(8,128)}) fusion(f32[2,577]{1,0:T(2,128)S(1)} %copy-done.20, f32[2,577]{1,0:T(2,128)S(1)} %copy-done.18, bf16[2,1,577,1024]{3,0,2,1:T(2,128)(2,1)} %param.12, f32[1024]{0:T(1024)S(1)} %copy-done.22, ...), kind=kOutput, calls=%fused_computation.58 | convolution fusion | flops 7272153088 | bytes 20502560 | tf_op jit(solution)/shard_map/bsn,kn->bsk/dot_general | solution.py:159
  658.9 41.7 %psum.7 = f32[12288]{0:T(1024)S(1)} all-reduce(f32[12288]{0:T(1024)S(1)} %constant_dynamic-update-slice_fusion.6), channel_id=1, replica_groups=mesh['dp'=8,'mp'=4] {'dp','mp'}, use_global_device_ids=true, to_apply=%region_18.19 | all-reduce | flops 12288 | bytes 98304 | tf_op jit(solution)/shard_map/psum | solution.py:307
  700.6 16.0 %fusion.39 = bf16[2,1,577,1024]{3,2,0,1:T(8,128)(2,1)S(1)} fusion(f32[2,577,1024]{2,1,0:T(8,128)} %copy-done.5, f32[1024]{0:T(1024)S(1)} %copy-done.24, pred[2]{0:T(512)(128)(4,1)S(1)} %copy-done.28, bf16[2,577,4096]{2,1,0:T(8,128)(2,1)} %copy-done.9, bf16[4096,1024,1]{1,0,2:T(8,128)(2,1)} %reshape.233), kind=kOutput, calls=%fused_computation.79 | convolution fusion | flops 9685180416 | bytes 24936450 | tf_op jit(solution)/shard_map/bsk,kn->bsn/dot_general | solution.py:155
  716.7 3.8 copy.76
  720.6 5.1 fusion.27
  725.7 9.4 copy.77
  740.2 103.8 %reduce-scatter.9.cloned.1.call-done = bf16[1,128,1024]{2,1,0:T(8,128)(2,1)} async-done(((bf16[32,128,1024]{2,1,0:T(8,128)(2,1)}), bf16[1,128,1024]{2,1,0:T(8,128)(2,1)}) %reduce-scatter.9.cloned.1.call-update) | async-done | bytes 262160 | tf_op jit(solution)/shard_map/reduce_scatter | solution.py:266
  843.9 1.8 bitcast_convert_fusion.5
  845.7 185.0 %reduce-scatter.11.cloned.1.call-done = bf16[1,1024,128]{2,1,0:T(8,128)(2,1)} async-done(((bf16[32,1024,128]{2,1,0:T(8,128)(2,1)}), bf16[1,1024,128]{2,1,0:T(8,128)(2,1)}) %reduce-scatter.11.cloned.1.call-update) | async-done | bytes 262160 | tf_op jit(solution)/shard_map/reduce_scatter | solution.py:252
  (141 shorter events, 21.5 us)
Async XLA Ops:
  7.2 83.0 %copy-start.1 = (bf16[2,1,577,1024]{3,0,2,1:T(2,128)(2,1)S(1)}, bf16[2,1,577,1024]{3,0,2,1:T(2,128)(2,1)}, u32[]{:S(2)}) copy-start(bf16[2,1,577,1024]{3,0,2,1:T(2,128)(2,1)} %param.12) | copy-start | bytes 7090180
  7.2 87.9 %all-gather.13.cloned.1.call-start = ((), (), s32[]{:S(2)}) async-start(), calls=%async_computation.9 | async-start | bytes 2162688 | tf_op jit(solution)/shard_map/all_gather | solution.py:197
  7.9 133.7 %all-gather.11.cloned.1.call-start = ((), (), s32[]{:S(2)}) async-start(), calls=%async_computation.8 | async-start | bytes 6488064 | tf_op jit(solution)/shard_map/all_gather | solution.py:196
  8.7 212.3 %all-gather.15.cloned.1.call-start = ((), (), s32[]{:S(2)}) async-start(), calls=%async_computation.10 | async-start | bytes 8650752 | tf_op jit(solution)/shard_map/all_gather | solution.py:198
  9.4 290.5 %all-gather.17.cloned.1.call-start = ((), (), s32[]{:S(2)}) async-start(), calls=%async_computation.11 | async-start | bytes 8650752 | tf_op jit(solution)/shard_map/all_gather | solution.py:199
  10.0 727.0 %reduce-scatter.7.cloned.1.call-start = ((), (), s32[]{:S(2)}) async-start(), calls=%async_computation.5 | async-start | bytes 2162688 | tf_op jit(solution)/shard_map/reduce_scatter | solution.py:278
  86.9 4.8 copy-start.10
  87.8 7.3 copy-start.27
  90.2 73.4 %copy-start.17 = (f32[2,577]{1,0:T(2,128)}, f32[2,577]{1,0:T(2,128)S(1)}, u32[]{:S(2)}) copy-start(f32[2,577]{1,0:T(2,128)S(1)} %broadcast_multiply_fusion.5) | copy-start | bytes 13852
  91.1 72.5 %copy-start.19 = (f32[2,577]{1,0:T(2,128)}, f32[2,577]{1,0:T(2,128)S(1)}, u32[]{:S(2)}) copy-start(f32[2,577]{1,0:T(2,128)S(1)} %add_rsqrt_fusion.1) | copy-start | bytes 13852
  91.7 71.9 %copy-start.21 = (f32[1024]{0:T(1024)}, f32[1024]{0:T(1024)S(1)}, u32[]{:S(2)}) copy-start(f32[1024]{0:T(1024)S(1)} %get-tuple-element.83) | copy-start | bytes 12292
  91.7 71.9 %copy-start.25 = (f32[1024]{0:T(1024)}, f32[1024]{0:T(1024)S(1)}, u32[]{:S(2)}) copy-start(f32[1024]{0:T(1024)S(1)} %get-tuple-element.82) | copy-start | bytes 12292
  175.0 32.4 %copy-start = (bf16[2,577,3072]{2,1,0:T(8,128)(2,1)}, bf16[2,577,3072]{2,1,0:T(8,128)(2,1)S(1)}, u32[]{:S(2)}) copy-start(bf16[2,577,3072]{2,1,0:T(8,128)(2,1)S(1)} %add_convert_fusion.query_ref.key_ref.value_ref) | copy-start | bytes 21270532
  175.0 32.4 %copy-start.2 = (bf16[2,1,577,1024]{3,0,2,1:T(2,128)(2,1)S(1)}, bf16[2,1,577,1024]{3,0,2,1:T(2,128)(2,1)}, u32[]{:S(2)}) copy-start(bf16[2,1,577,1024]{3,0,2,1:T(2,128)(2,1)} %param.12) | copy-start | bytes 7090180
  175.0 32.4 %copy-start.13 = (bf16[1024,1024,1]{1,0,2:T(8,128)(2,1)S(1)}, bf16[1024,1024,1]{1,0,2:T(8,128)(2,1)}, u32[]{:S(2)}) copy-start(bf16[1024,1024,1]{1,0,2:T(8,128)(2,1)} %reshape.231) | copy-start | bytes 6291460
  211.0 2.3 copy-start.5
  376.4 18.4 %copy-start.11 = (bf16[2,1,577,1024]{3,0,2,1:T(2,128)(2,1)S(1)}, bf16[2,1,577,1024]{3,0,2,1:T(2,128)(2,1)}, u32[]{:S(2)}) copy-start(bf16[2,1,577,1024]{3,0,2,1:T(2,128)(2,1)} %param.13) | copy-start | bytes 7090180
  376.4 18.4 %copy-start.28 = (pred[2]{0:T(512)(128)(4,1)S(1)}, pred[2]{0:T(512)(128)(4,1)}, u32[]{:S(2)}) copy-start(pred[2]{0:T(512)(128)(4,1)} %copy-done.27) | copy-start | bytes 10
  399.9 3.2 copy-start.6
  403.7 2.1 copy-start.14
  405.7 332.8 %reduce-scatter.5.cloned.1.call-start = ((), (), s32[]{:S(2)}) async-start(), calls=%async_computation.4 | async-start | bytes 6488064 | tf_op jit(solution)/shard_map/reduce_scatter | solution.py:290
  472.0 1.7 copy-start.7
  472.2 4.6 copy-start.3
  472.2 4.6 copy-start.18
  472.2 4.6 copy-start.20
  472.2 4.6 copy-start.22
  472.2 4.6 copy-start.26
  473.9 2.9 copy-start.15
  508.6 335.3 %reduce-scatter.9.cloned.1.call-start = ((), (), s32[]{:S(2)}) async-start(), calls=%async_computation.6 | async-start | bytes 8650752 | tf_op jit(solution)/shard_map/reduce_scatter | solution.py:266
  551.4 479.3 %reduce-scatter.11.cloned.1.call-start = ((), (), s32[]{:S(2)}) async-start(), calls=%async_computation.7 | async-start | bytes 8650752 | tf_op jit(solution)/shard_map/reduce_scatter | solution.py:252
  551.4 51.0 %copy-start.12 = (bf16[2,1,577,1024]{3,0,2,1:T(2,128)(2,1)S(1)}, bf16[2,1,577,1024]{3,0,2,1:T(2,128)(2,1)}, u32[]{:S(2)}) copy-start(bf16[2,1,577,1024]{3,0,2,1:T(2,128)(2,1)} %param.13) | copy-start | bytes 7090180
  598.7 3.7 copy-start.9
  641.9 16.6 %copy-start.8 = (bf16[2,577,1024]{2,1,0:T(8,128)(2,1)S(1)}, bf16[2,577,1024]{2,1,0:T(8,128)(2,1)}, u32[]{:S(2)}) copy-start(bf16[2,577,1024]{2,1,0:T(8,128)(2,1)} %get-tuple-element.20) | copy-start | bytes 7090180
  657.9 0.9 copy-start.23
  657.9 42.7 %copy-start.24 = (f32[1024]{0:T(1024)S(1)}, f32[1024]{0:T(1024)}, u32[]{:S(2)}) copy-start(f32[1024]{0:T(1024)} %get-tuple-element.79) | copy-start | bytes 12292
  658.0 62.5 %slice-start = ((s8[4784128]{0:T(1024)(128)(4,1)}), s8[589824]{0:T(1024)(128)(4,1)S(1)}, s32[]{:S(2)}) async-start(s8[4784128]{0:T(1024)(128)(4,1)} %bitcast.186), calls=%async_computation.12 | async-start | bytes 1179648
  700.6 16.0 %copy-start.16 = (f32[12288]{0:T(1024)}, f32[12288]{0:T(1024)S(1)}, u32[]{:S(2)}) copy-start(f32[12288]{0:T(1024)S(1)} %psum.7) | copy-start | bytes 147460
  700.6 19.9 %slice-start.1 = ((s8[4784128]{0:T(1024)(128)(4,1)}), s8[4194304]{0:T(1024)(128)(4,1)S(1)}, s32[]{:S(2)}) async-start(s8[4784128]{0:T(1024)(128)(4,1)} %bitcast.186), calls=%async_computation.13 | async-start | bytes 8388608
  716.7 3.9 copy-start.4
  725.7 9.5 slice-start.2
  725.7 9.5 slice-start.4
  725.7 9.5 slice-start.3
Sparse Core Ops, SparseCore 0:
  10.9 59.5 all-gather.12
  73.4 68.1 all-gather.10
  144.5 76.4 all-gather.14
  223.7 76.1 all-gather.16
  405.8 135.0 reduce-scatter.6
  547.4 110.6 reduce-scatter.4
  660.4 183.5 reduce-scatter.8
  846.2 184.4 reduce-scatter.10
